TPU v7x, 32 devices: a whole 2x2x4 slice. The times are simulated.
32 devices in a mesh: dp: 8 (over y, x, core), mp: 4 (over z).
Axes of the slice: x: 2, y: 2, z: 4, core: 2. Of those that a mesh axis runs over, the one named last changes fastest.
Arguments:
- inputs: bfloat16 [8192, 3072], P(('dp', 'mp')), may hold values from -64 to 64, as said below
- w_qkv: bfloat16 [3072, 3, 3072], P('dp', None, 'mp'), may hold values from -2 to 2
- w_out: bfloat16 [3072, 3072], P('mp', 'dp'), may hold values from -0.109375 to 0.109375
- upstream: bfloat16 [8192, 3072], P(('dp', 'mp')), may hold values from -6 to 6
Outputs:
- layer_out: bfloat16 [8192, 3072], P(('dp', 'mp'))
- grad_x: bfloat16 [8192, 3072], P(('dp', 'mp'))
- grad_wqkv: bfloat16 [3072, 3, 3072], P('dp', None, 'mp')
- grad_wout: bfloat16 [3072, 3072], P('mp', 'dp')
Inputs may be any that keep to these rules, and one draw needn't show every extreme that they name: `inputs`: Activations; each row's scale may differ.
All inputs are finite; a program needn't handle non-finite values.
Results may differ from a plain program's by a relative error of at most 0.014.
The roundings to bfloat16 on the way count: a program that leaves them out, or rounds other values in their place, can miss the bound.
Values may be sent and summed in bfloat16 or wider, within the bound.
A program may use at most 128 MiB of HBM per device.

v0:
```python
import jax
import jax.numpy as jnp
from jax import lax
from jax.sharding import PartitionSpec as P

HD = 128
PATCH = 256


epsilon = 1e-06


def rounded(values):
    return lax.optimization_barrier(values.astype(jnp.bfloat16)).astype(jnp.float32)


def fetch_weights(w_qkv, w_out):
    return (
        lax.all_gather(w_qkv, "dp", axis=0, tiled=True),
        lax.all_gather(w_out, "dp", axis=1, tiled=True),
    )


def per_device(inputs, w_qkv, w_out, upstream):
    local_rows, width = inputs.shape
    head_dim = HD
    local_width = w_qkv.shape[2]
    local_heads = local_width // head_dim
    inputs_float = inputs.astype(jnp.float32)
    centred = inputs_float - jnp.mean(inputs_float, axis=1, keepdims=True)
    inv_scale = lax.rsqrt(jnp.mean(centred * centred, axis=1, keepdims=True) + epsilon)
    standard = centred * inv_scale
    normed_local = standard.astype(jnp.bfloat16)
    normed, cotangent = (
        lax.all_gather(normed_local, "mp", axis=0, tiled=True),
        lax.all_gather(upstream, "mp", axis=0, tiled=True),
    )
    group_rows = normed.shape[0]
    images = group_rows // PATCH
    qkv_rows, out_cols = fetch_weights(w_qkv, w_out)
    qkv_matrix = qkv_rows.reshape(width, 3 * local_width)
    projected = jnp.dot(normed, qkv_matrix, preferred_element_type=jnp.float32).astype(jnp.bfloat16)
    split_view = projected.reshape(images, PATCH, 3, local_heads, head_dim)
    queries = split_view[:, :, 0]
    keys_part = split_view[:, :, 1]
    values_part = split_view[:, :, 2]
    scale = head_dim ** (-0.5)
    scores = (
        jnp.einsum("bqhe,bkhe->bhqk", queries, keys_part, preferred_element_type=jnp.float32)
        * scale
    )
    probs = jax.nn.softmax(scores, axis=-1)
    probs16 = probs.astype(jnp.bfloat16)
    context = jnp.einsum(
        "bhqk,bkhe->bqhe", probs16, values_part, preferred_element_type=jnp.float32
    )
    context = context.astype(jnp.bfloat16).reshape(group_rows, local_width)
    block = context
    attended = lax.psum_scatter(
        rounded(jnp.dot(block, out_cols, preferred_element_type=jnp.float32)).astype(jnp.bfloat16),
        "mp",
        scatter_dimension=0,
        tiled=True,
    ).astype(jnp.float32)
    layer_out = (inputs_float + attended).astype(jnp.bfloat16)
    qkv_again, out_again, _ = lax.optimization_barrier((w_qkv, w_out, attended))
    qkv_rows, out_cols = fetch_weights(qkv_again, out_again)
    qkv_matrix = qkv_rows.reshape(width, 3 * local_width)
    grad_context = lax.dot_general(
        cotangent, out_cols, (((1,), (1,)), ((), ())), preferred_element_type=jnp.float32
    ).astype(jnp.bfloat16)
    out_grad_term = rounded(
        lax.dot_general(
            context, cotangent, (((0,), (0,)), ((), ())), preferred_element_type=jnp.float32
        )
    )
    grad_heads = grad_context.reshape(images, PATCH, local_heads, head_dim)
    grad_probs = jnp.einsum(
        "bqhe,bkhe->bhqk", grad_heads, values_part, preferred_element_type=jnp.float32
    )
    grad_values = jnp.einsum(
        "bhqk,bqhe->bkhe", probs16, grad_heads, preferred_element_type=jnp.float32
    ).astype(jnp.bfloat16)
    row_totals = jnp.sum(probs * grad_probs, axis=-1, keepdims=True)
    grad_scores = (probs * (grad_probs - row_totals) * scale).astype(jnp.bfloat16)
    grad_queries = jnp.einsum(
        "bhqk,bkhe->bqhe", grad_scores, keys_part, preferred_element_type=jnp.float32
    ).astype(jnp.bfloat16)
    grad_keys = jnp.einsum(
        "bhqk,bqhe->bkhe", grad_scores, queries, preferred_element_type=jnp.float32
    ).astype(jnp.bfloat16)
    grad_projected = jnp.stack([grad_queries, grad_keys, grad_values], axis=2).reshape(
        group_rows, 3 * local_width
    )
    block = grad_projected
    grad_normed = lax.psum_scatter(
        rounded(
            lax.dot_general(
                block, qkv_matrix, (((1,), (1,)), ((), ())), preferred_element_type=jnp.float32
            )
        ).astype(jnp.bfloat16),
        "mp",
        scatter_dimension=0,
        tiled=True,
    ).astype(jnp.float32)
    centre_grad = jnp.mean(grad_normed, axis=1, keepdims=True)
    along = jnp.mean(grad_normed * standard, axis=1, keepdims=True)
    grad_x = (
        upstream.astype(jnp.float32) + inv_scale * (grad_normed - centre_grad - standard * along)
    ).astype(jnp.bfloat16)
    qkv_grad_term = rounded(
        lax.dot_general(
            normed, grad_projected, (((0,), (0,)), ((), ())), preferred_element_type=jnp.float32
        )
    )
    qkv_grad_term = qkv_grad_term.reshape(width, 3, local_width)
    qkv_grad_sum, out_grad_sum = (
        lax.psum_scatter(
            qkv_grad_term.astype(jnp.bfloat16), "dp", scatter_dimension=0, tiled=True
        ).astype(jnp.float32),
        lax.psum_scatter(
            out_grad_term.astype(jnp.bfloat16), "dp", scatter_dimension=1, tiled=True
        ).astype(jnp.float32),
    )
    return (layer_out, grad_x, qkv_grad_sum.astype(jnp.bfloat16), out_grad_sum.astype(jnp.bfloat16))


def solution(mesh):
    in_specs = (P(("dp", "mp"), None), P("dp", None, "mp"), P("mp", "dp"), P(("dp", "mp"), None))
    out_specs = (P(("dp", "mp"), None), P(("dp", "mp"), None), P("dp", None, "mp"), P("mp", "dp"))
    return jax.shard_map(
        per_device, mesh=mesh, in_specs=in_specs, out_specs=out_specs, check_vma=False
    )
```

profile of v0, /device:TPU:0, one launch (start us, length us, event | category | flops | bytes accessed | tf_op | source)
XLA Modules:
  0.0 896.8 jit_solution(893249508503789739)
XLA Ops:
  20.2 111.5 %all-gather.7.cloned.1.call-done = bf16[1024,3072]{1,0:T(8,128)(2,1)} async-done(((bf16[256,3072]{1,0:T(8,128)(2,1)}), bf16[1024,3072]{1,0:T(8,128)(2,1)}) %all-gather.7.cloned.1.call-update) | async-done | bytes 6291472 | tf_op jit(solution)/shard_map/all_gather | solution.py:35
  131.7 82.2 %all-gather.9.cloned.1.call-done = bf16[3072,3,768]{0,2,1:T(8,128)(2,1)} async-done(((bf16[384,3,768]{0,2,1:T(8,128)(2,1)}), bf16[3072,3,768]{0,2,1:T(8,128)(2,1)}) %all-gather.9.cloned.1.call-update) | async-done | bytes 14155792 | tf_op jit(solution)/shard_map/all_gather | solution.py:19
  213.9 20.7 %convolution_convert_fusion.3 = bf16[1024,2304]{1,0:T(8,128)(2,1)} fusion(bf16[1024,3072]{1,0:T(8,128)(2,1)} %all-gather.7.cloned.1.call-done, bf16[3072,2304]{0,1:T(8,128)(2,1)} %bitcast.79), kind=kOutput, calls=%fused_computation.9 | convolution fusion | flops 14497873920 | bytes 25165824 | tf_op jit(solution)/shard_map/dot_general | solution.py:42
  234.6 6.7 copy.41
  241.3 8.9 reshape.52
  263.6 4.8 fusion.67
  273.7 57.2 %all-gather.15.cloned.1.call-done = bf16[1024,3072]{1,0:T(8,128)(2,1)} async-done(((bf16[256,3072]{1,0:T(8,128)(2,1)}), bf16[1024,3072]{1,0:T(8,128)(2,1)}) %all-gather.15.cloned.1.call-update) | async-done | bytes 6291472 | tf_op jit(solution)/shard_map/all_gather | solution.py:36
  330.9 9.1 %convolution_convert_fusion.4 = bf16[768,3072]{1,0:T(8,128)(2,1)} fusion(bf16[1024,768]{0,1:T(8,128)(2,1)} %bitcast.75, bf16[1024,3072]{1,0:T(8,128)(2,1)} %all-gather.15.cloned.1.call-done), kind=kOutput, calls=%fused_computation.12 | convolution fusion | flops 4834197504 | bytes 12582912 | tf_op jit(solution)/shard_map/dot_general | solution.py:73
  339.9 6.7 copy.68
  346.9 23.7 %all-gather.13.cloned.1.call-done = bf16[768,3072]{1,0:T(8,128)(2,1)} async-done(((bf16[768,384]{1,0:T(8,128)(2,1)}), bf16[768,3072]{1,0:T(8,128)(2,1)}) %all-gather.13.cloned.1.call-update) | async-done | bytes 4718608 | tf_op jit(solution)/shard_map/all_gather | solution.py:20
  370.6 9.5 %fusion.41 = bf16[1024,768]{0,1:T(8,128)(2,1)} fusion(bf16[768,3072]{1,0:T(8,128)(2,1)} %all-gather.13.cloned.1.call-done, bf16[1024,3072]{1,0:T(8,128)(2,1)} %all-gather.15.cloned.1.call-done), kind=kOutput, calls=%fused_computation.50 | convolution fusion | flops 4832624640 | bytes 12582912 | tf_op jit(solution)/shard_map/dot_general | solution.py:69
  384.1 5.1 fusion.58
  389.2 12.0 %fusion.53 = bf16[4,256,1,6,128]{1,4,3,0,2:T(8,128)(2,1)} fusion(f32[4,6,256,256]{2,3,1,0:T(8,128)} %fusion.58, bf16[4,256,1,6,128]{4,1,3,0,2:T(8,128)(2,1)} %copy.74, f32[4,6,256,256]{2,3,1,0:T(8,128)} %copy-done.4, f32[4,6,256]{2,1,0:T(8,128)S(1)} %get-tuple-element.23), kind=kOutput, calls=%fused_computation.54 | convolution fusion | flops 414456064 | bytes 15753216 | tf_op jit(solution)/shard_map/bhqk,bkhe->bqhe/dot_general | solution.py:86
  401.3 12.4 %fusion.48 = bf16[4,256,1,6,128]{1,4,3,0,2:T(8,128)(2,1)} fusion(f32[4,6,256,256]{2,3,1,0:T(8,128)} %fusion.58, bf16[4,256,1,6,128]{4,1,3,0,2:T(8,128)(2,1)S(1)} %copy.73, f32[4,6,256,256]{2,3,1,0:T(8,128)} %copy-done.4, f32[4,6,256]{2,1,0:T(8,128)S(1)} %get-tuple-element.23), kind=kOutput, calls=%fused_computation.53 | convolution fusion | flops 414456064 | bytes 15753216 | tf_op jit(solution)/shard_map/bhqk,bqhe->bkhe/dot_general | solution.py:89
  426.9 27.0 %all-gather.17.cloned.1.call-done = bf16[3072,3,768]{0,2,1:T(8,128)(2,1)} async-done(((bf16[384,3,768]{0,2,1:T(8,128)(2,1)}), bf16[3072,3,768]{0,2,1:T(8,128)(2,1)}) %all-gather.17.cloned.1.call-update) | async-done | bytes 14155792 | tf_op jit(solution)/shard_map/all_gather | solution.py:19
  453.9 20.7 %convolution_convert_fusion.2 = bf16[1024,3072]{1,0:T(8,128)(2,1)} fusion(bf16[1024,2304]{0,1:T(8,128)(2,1)} %bitcast.73, bf16[3072,2304]{0,1:T(8,128)(2,1)} %bitcast.78), kind=kOutput, calls=%fused_computation.8 | convolution fusion | flops 14498660352 | bytes 25165824 | tf_op jit(solution)/shard_map/dot_general | solution.py:98
  474.6 20.7 %all-gather.11.cloned.1.call-done = bf16[768,3072]{1,0:T(8,128)(2,1)} async-done(((bf16[768,384]{1,0:T(8,128)(2,1)}), bf16[768,3072]{1,0:T(8,128)(2,1)}) %all-gather.11.cloned.1.call-update) | async-done | bytes 4718608 | tf_op jit(solution)/shard_map/all_gather | solution.py:20
  495.4 9.5 %convolution_convert_fusion.1 = bf16[1024,3072]{1,0:T(8,128)(2,1)} fusion(bf16[1024,768]{0,1:T(8,128)(2,1)S(1)} %bitcast.76, bf16[768,3072]{1,0:T(8,128)(2,1)} %all-gather.11.cloned.1.call-done), kind=kOutput, calls=%fused_computation.7 | convolution fusion | flops 4834983936 | bytes 12582912 | tf_op jit(solution)/shard_map/dot_general | solution.py:60
  505.0 22.0 %convolution_convert_fusion = bf16[3072,2304]{1,0:T(8,128)(2,1)} fusion(bf16[1024,3072]{1,0:T(8,128)(2,1)} %all-gather.7.cloned.1.call-done, bf16[1024,2304]{0,1:T(8,128)(2,1)} %bitcast.74), kind=kOutput, calls=%fused_computation.2 | convolution fusion | flops 14502592512 | bytes 25165824 | tf_op jit(solution)/shard_map/dot_general | solution.py:112
  527.0 25.7 %reduce-scatter.15.cloned.1.call-done = bf16[384,768]{1,0:T(8,128)(2,1)} async-done(((bf16[3072,768]{1,0:T(8,128)(2,1)}), bf16[384,768]{1,0:T(8,128)(2,1)}) %reduce-scatter.15.cloned.1.call-update) | async-done | bytes 589840
  554.8 111.1 %reduce-scatter.11.cloned.1.call-done = bf16[256,3072]{1,0:T(8,128)(2,1)} async-done(((bf16[1024,3072]{1,0:T(8,128)(2,1)}), bf16[256,3072]{1,0:T(8,128)(2,1)}) %reduce-scatter.11.cloned.1.call-update) | async-done | bytes 1572880 | tf_op jit(solution)/shard_map/reduce_scatter | solution.py:96
  668.3 111.3 %reduce-scatter.9.cloned.1.call-done = bf16[256,3072]{1,0:T(8,128)(2,1)} async-done(((bf16[1024,3072]{1,0:T(8,128)(2,1)}), bf16[256,3072]{1,0:T(8,128)(2,1)}) %reduce-scatter.9.cloned.1.call-update) | async-done | bytes 1572880 | tf_op jit(solution)/shard_map/reduce_scatter | solution.py:59
  779.6 5.5 fusion.21
  785.1 99.7 %reduce-scatter.13.cloned.1.call-done = bf16[384,2304]{1,0:T(8,128)(2,1)} async-done(((bf16[3072,2304]{1,0:T(8,128)(2,1)}), bf16[384,2304]{1,0:T(8,128)(2,1)}) %reduce-scatter.13.cloned.1.call-update) | async-done | bytes 1769488
  (70 shorter events, 58.8 us)
Async XLA Ops:
  7.2 4.6 copy-start
  7.2 124.5 %all-gather.7.cloned.1.call-start = ((), (), s32[]{:S(2)}) async-start(), calls=%async_computation.4 | async-start | bytes 7864320 | tf_op jit(solution)/shard_map/all_gather | solution.py:35
  9.0 2.1 copy-start.9
  9.0 4.5 copy-start.3
  11.2 0.6 copy-start.11
  13.5 200.4 %all-gather.9.cloned.1.call-start = ((), (), s32[]{:S(2)}) async-start(), calls=%async_computation.5 | async-start | bytes 15925248 | tf_op jit(solution)/shard_map/all_gather | solution.py:19
  15.8 315.1 %all-gather.15.cloned.1.call-start = ((), (), s32[]{:S(2)}) async-start(), calls=%async_computation.9 | async-start | bytes 7864320 | tf_op jit(solution)/shard_map/all_gather | solution.py:36
  16.5 354.1 %all-gather.13.cloned.1.call-start = ((), (), s32[]{:S(2)}) async-start(), calls=%async_computation.8 | async-start | bytes 5308416 | tf_op jit(solution)/shard_map/all_gather | solution.py:20
  17.1 436.7 %all-gather.17.cloned.1.call-start = ((), (), s32[]{:S(2)}) async-start(), calls=%async_computation.10 | async-start | bytes 15925248 | tf_op jit(solution)/shard_map/all_gather | solution.py:19
  19.4 475.9 %all-gather.11.cloned.1.call-start = ((), (), s32[]{:S(2)}) async-start(), calls=%async_computation.6 | async-start | bytes 5308416 | tf_op jit(solution)/shard_map/all_gather | solution.py:20
  20.0 532.7 %reduce-scatter.15.cloned.1.call-start = ((), (), s32[]{:S(2)}) async-start(), calls=%async_computation.13 | async-start | bytes 5308416
  268.4 2.6 copy-start.4
  346.6 319.2 %reduce-scatter.11.cloned.1.call-start = ((), (), s32[]{:S(2)}) async-start(), calls=%async_computation.11 | async-start | bytes 7864320 | tf_op jit(solution)/shard_map/reduce_scatter | solution.py:96
  401.3 12.4 %copy-start.2 = (bf16[4,256,6,128]{1,0,3,2:T(4,128)(2,1)S(1)}, bf16[4,256,6,128]{1,0,3,2:T(4,128)(2,1)}, u32[]{:S(2)}) copy-start(bf16[4,256,6,128]{1,0,3,2:T(4,128)(2,1)} %reshape.54) | copy-start | bytes 4718596
  413.7 4.4 copy-start.6
  413.7 4.4 copy-start.7
  474.6 20.8 %copy-start.8 = (bf16[96,8,4,256]{3,1,2,0:T(8,128)(2,1)S(1)}, bf16[96,8,4,256]{3,1,2,0:T(8,128)(2,1)}, u32[]{:S(2)}) copy-start(bf16[96,8,4,256]{3,1,2,0:T(8,128)(2,1)} %copy.75) | copy-start | bytes 4718596
  474.6 305.0 %reduce-scatter.9.cloned.1.call-start = ((), (), s32[]{:S(2)}) async-start(), calls=%async_computation.7 | async-start | bytes 7864320 | tf_op jit(solution)/shard_map/reduce_scatter | solution.py:59
  504.9 379.9 %reduce-scatter.13.cloned.1.call-start = ((), (), s32[]{:S(2)}) async-start(), calls=%async_computation.12 | async-start | bytes 15925248
  527.0 138.9 %copy-start.1 = (bf16[256,3072]{1,0:T(8,128)(2,1)S(1)}, bf16[256,3072]{1,0:T(8,128)(2,1)}, u32[]{:S(2)}) copy-start(bf16[256,3072]{1,0:T(8,128)(2,1)} %param.4) | copy-start | bytes 4718596
  527.0 138.9 %copy-start.10 = (f32[256]{0:T(256)S(1)}, f32[256]{0:T(256)}, u32[]{:S(2)}) copy-start(f32[256]{0:T(256)} %copy-done.9) | copy-start | bytes 3076
  527.0 138.9 %copy-start.12 = (f32[256]{0:T(256)S(1)}, f32[256]{0:T(256)}, u32[]{:S(2)}) copy-start(f32[256]{0:T(256)} %copy-done.11) | copy-start | bytes 3076
  527.0 252.6 %copy-start.5 = (bf16[256,3072]{1,0:T(8,128)(2,1)S(1)}, bf16[256,3072]{1,0:T(8,128)(2,1)}, u32[]{:S(2)}) copy-start(bf16[256,3072]{1,0:T(8,128)(2,1)} %param.7) | copy-start | bytes 4718596
Sparse Core Ops, SparseCore 0:
  13.6 118.0 all-gather.6
  134.1 79.7 all-gather.8
  215.5 115.3 all-gather.14
  332.6 37.9 all-gather.12
  372.3 81.4 all-gather.16
  455.6 39.7 all-gather.10
  498.8 53.8 reduce-scatter.14
  555.1 110.7 reduce-scatter.10
  668.3 111.2 reduce-scatter.8
  783.5 101.2 reduce-scatter.12
where the time goes:
time: 900 us; the launch traced here: 897 us
  waiting for transfers between devices  672 us (75%)
  matrix products  129 us (14%)
  local copies, waits for them, and re-layouts  61.8 us (7%)
  other arithmetic  19.3 us (2%)
  between operations  14.5 us (2%)
    unnamed x12, waiting for transfers between devices  127 us
    all_gather x1, waiting for transfers between devices, per_device(): lax.all_gather(normed_local, 'mp', axis=0, tiled=True)  111 us
    reduce_scatter x1, waiting for transfers between devices, per_device(): lax.psum_scatter(rounded(jnp.dot(block, out_cols, preferred_element_type=...  111 us
    reduce_scatter x1, waiting for transfers between devices, per_device(): lax.psum_scatter(rounded(lax.dot_general(block, qkv_matrix, (((1,), (1,))...  111 us
    all_gather x2, waiting for transfers between devices, fetch_weights(): lax.all_gather(w_qkv, 'dp', axis=0, tiled=True)  109 us
    all_gather x1, waiting for transfers between devices, per_device(): lax.all_gather(upstream, 'mp', axis=0, tiled=True)  57.2 us
    all_gather x2, waiting for transfers between devices, fetch_weights(): lax.all_gather(w_out, 'dp', axis=1, tiled=True)  44.4 us
    unnamed x35, local copies, waits for them, and re-layouts  30.2 us
  transfers between devices with their start and end apart: 10, of which 10 were waited for; matrix products, arithmetic and copies ran while one was open for 22% of the time, Pallas kernels for 0%

commit v1 on v0

v1 whole, which is shorter than its diff:
```python
import functools

import jax
import jax.numpy as jnp
from jax import lax
from jax.experimental import pallas as pl
from jax.experimental.pallas import tpu as pltpu
from jax.sharding import PartitionSpec as P

HD = 128
PATCH = 256
SCALE = HD ** (-0.5)
epsilon = 1e-06
VMEM_BYTES = 32 * 1024 * 1024

NT = (((1,), (1,)), ((), ()))
TN = (((0,), (0,)), ((), ()))
NN = (((1,), (0,)), ((), ()))


def dot(left, right, dims):
    return lax.dot_general(left, right, dims, preferred_element_type=jnp.float32)


def softmax_of(queries, keys):
    scores = dot(queries, keys, NT) * SCALE
    weights = jnp.exp(scores - jnp.max(scores, axis=-1, keepdims=True))
    return weights / jnp.sum(weights, axis=-1, keepdims=True)


def forward_kernel(projected_ref, context_ref):
    width = context_ref.shape[1]
    for low in range(0, width, HD):
        queries = projected_ref[:, low:low + HD]
        keys = projected_ref[:, width + low:width + low + HD]
        values = projected_ref[:, 2 * width + low:2 * width + low + HD]
        probs16 = softmax_of(queries, keys).astype(jnp.bfloat16)
        context_ref[:, low:low + HD] = dot(probs16, values, NN).astype(jnp.bfloat16)


def backward_kernel(projected_ref, grad_context_ref, grad_ref):
    width = grad_context_ref.shape[1]
    for low in range(0, width, HD):
        queries = projected_ref[:, low:low + HD]
        keys = projected_ref[:, width + low:width + low + HD]
        values = projected_ref[:, 2 * width + low:2 * width + low + HD]
        grad_heads = grad_context_ref[:, low:low + HD]
        probs = softmax_of(queries, keys)
        probs16 = probs.astype(jnp.bfloat16)
        grad_probs = dot(grad_heads, values, NT)
        row_totals = jnp.sum(probs * grad_probs, axis=-1, keepdims=True)
        grad_scores = (probs * (grad_probs - row_totals) * SCALE).astype(jnp.bfloat16)
        grad_ref[:, low:low + HD] = dot(grad_scores, keys, NN).astype(jnp.bfloat16)
        grad_ref[:, width + low:width + low + HD] = dot(grad_scores, queries, TN).astype(jnp.bfloat16)
        grad_ref[:, 2 * width + low:2 * width + low + HD] = dot(probs16, grad_heads, TN).astype(
            jnp.bfloat16
        )


def rows_spec(columns):
    return pl.BlockSpec((PATCH, columns), lambda image: (image, 0))


def attention_forward(projected):
    rows, width = projected.shape[0], projected.shape[1] // 3
    pairs = rows * width * PATCH // HD
    return pl.pallas_call(
        forward_kernel,
        grid=(rows // PATCH,),
        in_specs=[rows_spec(3 * width)],
        out_specs=rows_spec(width),
        out_shape=jax.ShapeDtypeStruct((rows, width), jnp.bfloat16),
        compiler_params=pltpu.CompilerParams(vmem_limit_bytes=VMEM_BYTES),
        cost_estimate=pl.CostEstimate(
            flops=4 * pairs * HD, bytes_accessed=8 * rows * width, transcendentals=pairs
        ),
        name="attention_forward",
    )(projected)


def attention_backward(projected, grad_context):
    rows, width = grad_context.shape
    pairs = rows * width * PATCH // HD
    return pl.pallas_call(
        backward_kernel,
        grid=(rows // PATCH,),
        in_specs=[rows_spec(3 * width), rows_spec(width)],
        out_specs=rows_spec(3 * width),
        out_shape=jax.ShapeDtypeStruct((rows, 3 * width), jnp.bfloat16),
        compiler_params=pltpu.CompilerParams(vmem_limit_bytes=VMEM_BYTES),
        cost_estimate=pl.CostEstimate(
            flops=10 * pairs * HD, bytes_accessed=14 * rows * width, transcendentals=pairs
        ),
        name="attention_backward",
    )(projected, grad_context)


def line_gather(block, axis, count):
    me = lax.axis_index(axis)
    right, left = [block], [block]
    for step in range(1, count):
        right.append(
            lax.ppermute(right[-1], axis, [(i, i + 1) for i in range(step - 1, count - 1)])
        )
        left.append(lax.ppermute(left[-1], axis, [(i, i - 1) for i in range(1, count - step + 1)]))
    blocks = [block]
    for k in range(1, count):
        blocks.append(jnp.where(me >= k, right[k], left[count - k]))
    return blocks, (right[-1], left[-1])


def line_scatter_sum(parts, axis, count):
    from_left = from_right = None
    for step in range(1, count):
        rightward, leftward = parts[step], parts[count - step]
        if step > 1:
            rightward = (rightward.astype(jnp.float32) + from_left.astype(jnp.float32)).astype(
                jnp.bfloat16
            )
            leftward = (leftward.astype(jnp.float32) + from_right.astype(jnp.float32)).astype(
                jnp.bfloat16
            )
        from_left = lax.ppermute(
            rightward, axis, [(i, i + 1) for i in range(0, min(step, count - 1))]
        )
        from_right = lax.ppermute(
            leftward, axis, [(i, i - 1) for i in range(max(count - step, 1), count)]
        )
    total = parts[0].astype(jnp.float32)
    if from_left is not None:
        total = total + from_left.astype(jnp.float32) + from_right.astype(jnp.float32)
    return total


def per_device(count, inputs, w_qkv, w_out, upstream):
    local_rows, width = inputs.shape
    local_width = w_qkv.shape[2]
    inputs_float = inputs.astype(jnp.float32)
    centred = inputs_float - jnp.mean(inputs_float, axis=1, keepdims=True)
    inv_scale = lax.rsqrt(jnp.mean(centred * centred, axis=1, keepdims=True) + epsilon)
    standard = centred * inv_scale
    normed_local = standard.astype(jnp.bfloat16)

    qkv_matrix = lax.all_gather(w_qkv, "dp", axis=0, tiled=True).reshape(width, 3 * local_width)
    out_turned = lax.all_gather(w_out.T, "dp", axis=0, tiled=True)

    def turned(blocks):
        if local_rows % PATCH == 0:
            return blocks
        stacked, me = jnp.stack(blocks), lax.axis_index("mp")
        return [
            lax.dynamic_index_in_dim(stacked, lax.rem(me + count - k, count), keepdims=False)
            for k in range(count)
        ]

    normed_blocks, last = line_gather(normed_local, "mp", count)
    normed = jnp.concatenate(turned(normed_blocks), axis=0)
    upstream_later, _, _ = lax.optimization_barrier((upstream,) + last)
    cotangent_blocks, _ = line_gather(upstream_later, "mp", count)
    cotangent = jnp.concatenate(turned(cotangent_blocks), axis=0)

    def by_block(rows):
        return turned([rows[k * local_rows:(k + 1) * local_rows] for k in range(count)])

    projected = dot(normed, qkv_matrix, NN).astype(jnp.bfloat16)
    context = attention_forward(projected)
    attended_parts = dot(context, out_turned, NT).astype(jnp.bfloat16)
    attended = line_scatter_sum(by_block(attended_parts), "mp", count)
    layer_out = (inputs_float + attended).astype(jnp.bfloat16)

    grad_context = dot(cotangent, out_turned, NN).astype(jnp.bfloat16)
    grad_projected = attention_backward(projected, grad_context)
    normed_parts = dot(grad_projected, qkv_matrix, NT).astype(jnp.bfloat16)
    grad_normed = line_scatter_sum(by_block(normed_parts), "mp", count)

    out_term = dot(cotangent, context, TN).astype(jnp.bfloat16)
    out_sum = lax.psum_scatter(out_term, "dp", scatter_dimension=0, tiled=True)
    qkv_term = dot(normed, grad_projected, TN).astype(jnp.bfloat16)
    qkv_sum = lax.psum_scatter(
        qkv_term.reshape(width, 3, local_width), "dp", scatter_dimension=0, tiled=True
    )

    centre_grad = jnp.mean(grad_normed, axis=1, keepdims=True)
    along = jnp.mean(grad_normed * standard, axis=1, keepdims=True)
    grad_x = (
        upstream.astype(jnp.float32) + inv_scale * (grad_normed - centre_grad - standard * along)
    ).astype(jnp.bfloat16)
    return (layer_out, grad_x, qkv_sum.astype(jnp.bfloat16), out_sum.T.astype(jnp.bfloat16))


def solution(mesh):
    in_specs = (P(("dp", "mp"), None), P("dp", None, "mp"), P("mp", "dp"), P(("dp", "mp"), None))
    out_specs = (P(("dp", "mp"), None), P(("dp", "mp"), None), P("dp", None, "mp"), P("mp", "dp"))
    return jax.shard_map(
        functools.partial(per_device, mesh.shape["mp"]),
        mesh=mesh,
        in_specs=in_specs,
        out_specs=out_specs,
        check_vma=False,
    )
```

time: 900 us -> 583 us (0.65)
  waiting for transfers between devices: 672 us -> 347 us
  starting transfers between devices: 0.79 us -> 50.8 us
  matrix products: 129 us -> 92.4 us
  local copies, waits for them, and re-layouts: 61.8 us -> 30.4 us
  Pallas kernels: 0 us -> 19.3 us
    ppermute x0 -> x24, waiting for transfers between devices: none -> 347 us  [the longest x6 189 us: line_gather(): lax.ppermute(left[-1], axis, [(i, i - 1) for i in range(1, count - step +...]
    all_gather x6 -> x2, waiting for transfers between devices: 322 us -> 0.02 us  [the longest x1 0.02 us: per_device(): out_turned = lax.all_gather(w_out.T, 'dp', axis=0, tiled=True)]
    reduce_scatter x2, waiting for transfers between devices: 222 us -> 0.01 us  [the longest x1 0.01 us: per_device(): out_sum = lax.psum_scatter(out_term, 'dp', scatter_dimension=0, tiled=True)]
    unnamed x12 -> x4, waiting for transfers between devices: 127 us -> 0.07 us
    ppermute x0 -> x24, starting transfers between devices: none -> 50.4 us  [the longest x6 22.2 us: line_scatter_sum(): lax.ppermute(rightward, axis, [(i, i + 1) for i in range(0, min(step, cou...]
    dot_general x12 -> x6, matrix products: 129 us -> 92.4 us  [dot(): lax.dot_general(left, right, dims, preferred_element_type=jnp.float32)]
    pallas_call x0 -> x2, Pallas kernels: none -> 19.3 us  [the longest x1 13.9 us: attention_backward(): pl.pallas_call(backward_kernel, grid=(rows // PATCH,), in_specs=[rows_spe...]
    unnamed x35 -> x50, local copies, waits for them, and re-layouts: 30.2 us -> 11.3 us
  transfers between devices with their start and end apart: 10 -> 28, of which waited for: 10 -> 12; matrix products, arithmetic and copies ran while one was open for 22% -> 24% of each run, Pallas kernels for 0% -> 3%
where the time goes in v1:
time: 583 us; the launch traced here: 577 us
  waiting for transfers between devices  347 us (60%)
  matrix products  92.4 us (16%)
  starting transfers between devices  50.8 us (9%)
  local copies, waits for them, and re-layouts  30.4 us (5%)
  other arithmetic  22.5 us (4%)
  Pallas kernels  19.3 us (3%)
  between operations  14.5 us (2%)
    ppermute x6, waiting for transfers between devices, line_gather(): lax.ppermute(left[-1], axis, [(i, i - 1) for i in range(1, count - step +...  189 us
    ppermute x6, waiting for transfers between devices, line_scatter_sum(): lax.ppermute(rightward, axis, [(i, i + 1) for i in range(0, min(step, cou...  158 us
    dot_general x6, matrix products, dot(): lax.dot_general(left, right, dims, preferred_element_type=jnp.float32)  92.4 us
    ppermute x6, starting transfers between devices, line_scatter_sum(): lax.ppermute(rightward, axis, [(i, i + 1) for i in range(0, min(step, cou...  22.2 us
    reshape x1, local copies, waits for them, and re-layouts, per_device(): qkv_term.reshape(width, 3, local_width)  18.7 us
    ppermute x6, starting transfers between devices, line_gather(): lax.ppermute(right[-1], axis, [(i, i + 1) for i in range(step - 1, count...  14.7 us
    pallas_call x1, Pallas kernels, attention_backward(): pl.pallas_call(backward_kernel, grid=(rows // PATCH,), in_specs=[rows_spe...  13.9 us
  transfers between devices with their start and end apart: 28, of which 12 were waited for; matrix products, arithmetic and copies ran while one was open for 24% of the time, Pallas kernels for 3%

profile of v1, /device:TPU:0, one launch (start us, length us, event | category | flops | bytes accessed | tf_op | source)
XLA Modules:
  0.0 577.0 jit_solution(5785143659325426907)
XLA Ops:
  14.1 5.7 collective-permute-start
  19.7 32.4 %collective-permute-done.1 = bf16[256,3072]{1,0:T(8,128)(2,1)S(1)} collective-permute-done((bf16[256,3072]{1,0:T(8,128)(2,1)S(1)}, bf16[256,3072]{1,0:T(8,128)(2,1)S(1)}, u32[]{:S(2)}, u32[]{:S(2)}) %collective-permute-start.1) | collective-permute-done | bytes 1572896 | tf_op jit(solution)/shard_map/ppermute | solution.py:105
  54.2 35.4 %collective-permute-done.2 = bf16[256,3072]{1,0:T(8,128)(2,1)S(1)} collective-permute-done((bf16[256,3072]{1,0:T(8,128)(2,1)S(1)}, bf16[256,3072]{1,0:T(8,128)(2,1)S(1)}, u32[]{:S(2)}, u32[]{:S(2)}) %collective-permute-start.2) | collective-permute-done | bytes 1572896 | tf_op jit(solution)/shard_map/ppermute | solution.py:105
  91.6 34.6 %collective-permute-done.3 = bf16[256,3072]{1,0:T(8,128)(2,1)S(1)} collective-permute-done((bf16[256,3072]{1,0:T(8,128)(2,1)S(1)}, bf16[256,3072]{1,0:T(8,128)(2,1)S(1)}, u32[]{:S(2)}, u32[]{:S(2)}) %collective-permute-start.3) | collective-permute-done | bytes 1572896 | tf_op jit(solution)/shard_map/ppermute | solution.py:105
  127.5 5.7 collective-permute-start.12
  133.4 28.7 %collective-permute-done.13 = bf16[256,3072]{1,0:T(8,128)(2,1)} collective-permute-done((bf16[256,3072]{1,0:T(8,128)(2,1)S(1)}, bf16[256,3072]{1,0:T(8,128)(2,1)}, u32[]{:S(2)}, u32[]{:S(2)}) %collective-permute-start.13) | collective-permute-done | bytes 1572896 | tf_op jit(solution)/shard_map/ppermute | solution.py:105
  168.4 28.7 %collective-permute-done.14 = bf16[256,3072]{1,0:T(8,128)(2,1)S(1)} collective-permute-done((bf16[256,3072]{1,0:T(8,128)(2,1)}, bf16[256,3072]{1,0:T(8,128)(2,1)S(1)}, u32[]{:S(2)}, u32[]{:S(2)}) %collective-permute-start.14) | collective-permute-done | bytes 1572896 | tf_op jit(solution)/shard_map/ppermute | solution.py:105
  202.0 28.9 %collective-permute-done.15 = bf16[256,3072]{1,0:T(8,128)(2,1)S(1)} collective-permute-done((bf16[256,3072]{1,0:T(8,128)(2,1)S(1)}, bf16[256,3072]{1,0:T(8,128)(2,1)S(1)}, u32[]{:S(2)}, u32[]{:S(2)}) %collective-permute-start.15) | collective-permute-done | bytes 1572896 | tf_op jit(solution)/shard_map/ppermute | solution.py:105
  235.3 25.7 %convolution_convert_fusion.3.projected_ref = bf16[1024,2304]{1,0:T(8,128)(2,1)} fusion(bf16[3072,2304]{0,1:T(8,128)(2,1)} %bitcast.15, bf16[256,3072]{1,0:T(8,128)(2,1)} %broadcast_select_fusion.1, bf16[256,3072]{1,0:T(8,128)(2,1)S(1)} %copy-done.8, bf16[256,3072]{1,0:T(8,128)(2,1)} %broadcast_select_fusion.5, bf16[256,3072]{1,0:T(8,128)(2,1)} %copy-done.19), kind=kOutput, calls=%fused_computation.5 | convolution fusion | flops 14523039744 | bytes 25165824 | tf_op jit(solution)/shard_map/dot_general | solution.py:22
  263.3 5.4 attention_forward.1
  268.8 6.9 %convolution_convert_fusion.4 = bf16[3072,768]{1,0:T(8,128)(2,1)} fusion(bf16[1024,768]{1,0:T(8,128)(2,1)S(1)} %attention_forward.1, bf16[256,3072]{1,0:T(8,128)(2,1)S(1)} %copy-done.18, bf16[256,3072]{1,0:T(8,128)(2,1)S(1)} %copy-done.16, bf16[256,3072]{1,0:T(8,128)(2,1)S(1)} %copy-done.17, bf16[256,3072]{1,0:T(8,128)(2,1)S(1)} %copy-done.5), kind=kOutput, calls=%fused_computation.6 | convolution fusion | flops 4859363328 | bytes 12582912 | tf_op jit(solution)/shard_map/dot_general | solution.py:22
  276.0 10.7 %convolution_convert_fusion.5.grad_context_ref = bf16[1024,768]{1,0:T(8,128)(2,1)S(1)} fusion(bf16[3072,768]{0,1:T(8,128)(2,1)} %all-gather.5.cloned.1.call-done, bf16[256,3072]{1,0:T(8,128)(2,1)} %broadcast_select_fusion, bf16[256,3072]{1,0:T(8,128)(2,1)} %broadcast_select_fusion.2, bf16[256,3072]{1,0:T(8,128)(2,1)} %broadcast_select_fusion.4, ...), kind=kOutput, calls=%fused_computation.35 | convolution fusion | flops 4857790464 | bytes 12582912 | tf_op jit(solution)/shard_map/dot_general | solution.py:22
  289.5 13.9 %attention_backward.1 = bf16[1024,2304]{1,0:T(8,128)(2,1)S(1)} custom-call(bf16[1024,2304]{1,0:T(8,128)(2,1)S(1)} %copy-done.1, bf16[1024,768]{1,0:T(8,128)(2,1)S(1)} %convolution_convert_fusion.5.grad_context_ref), custom_call_target="tpu_custom_call" | custom-call | flops 2013265920 | bytes 11010048 | tf_op jit(solution)/shard_map/attention_backward/pallas_call | solution.py:84
  303.4 22.3 %convolution_convert_fusion = bf16[3072,2304]{0,1:T(8,128)(2,1)} fusion(bf16[1024,2304]{1,0:T(8,128)(2,1)S(1)} %attention_backward.1, bf16[256,3072]{1,0:T(8,128)(2,1)} %broadcast_select_fusion.1, bf16[256,3072]{1,0:T(8,128)(2,1)S(1)} %copy-done.9, bf16[256,3072]{1,0:T(8,128)(2,1)} %broadcast_select_fusion.5, bf16[256,3072]{1,0:T(8,128)(2,1)} %copy-done.19), kind=kOutput, calls=%fused_computation | convolution fusion | flops 14527758336 | bytes 25165824 | tf_op jit(solution)/shard_map/dot_general | solution.py:22
  325.8 18.7 %copy.11 = bf16[3072,3,768]{2,0,1:T(8,128)(2,1)} copy(bf16[3072,3,768]{0,2,1:T(8,128)(2,1)} %bitcast.12) | data formatting | bytes 28311552 | tf_op jit(solution)/shard_map/reshape | solution.py:180
  344.4 18.9 %convolution_convert_fusion.2 = bf16[1024,3072]{1,0:T(8,128)(2,1)S(1)} fusion(bf16[1024,2304]{1,0:T(8,128)(2,1)} %copy-done.2, bf16[3072,2304]{0,1:T(8,128)(2,1)} %bitcast.16), kind=kOutput, calls=%fused_computation.4 | convolution fusion | flops 14498660352 | bytes 25165824 | tf_op jit(solution)/shard_map/dot_general | solution.py:22
  367.3 7.9 %convolution_convert_fusion.1 = bf16[1024,3072]{1,0:T(8,128)(2,1)S(1)} fusion(bf16[1024,768]{1,0:T(8,128)(2,1)S(1)} %attention_forward.1, bf16[3072,768]{0,1:T(8,128)(2,1)} %all-gather.5.cloned.1.call-done), kind=kOutput, calls=%fused_computation.3 | convolution fusion | flops 4834983936 | bytes 12582912 | tf_op jit(solution)/shard_map/dot_general | solution.py:22
  377.6 23.6 %collective-permute-done.18 = bf16[256,3072]{1,0:T(8,128)(2,1)S(1)} collective-permute-done((bf16[256,3072]{1,0:T(8,128)(2,1)S(1)}, bf16[256,3072]{1,0:T(8,128)(2,1)S(1)}, u32[]{:S(2)}, u32[]{:S(2)}) %collective-permute-start.18) | collective-permute-done | bytes 1572896 | tf_op jit(solution)/shard_map/ppermute | solution.py:123
  402.2 4.5 collective-permute-start.19
  407.5 27.5 %collective-permute-done.6 = bf16[256,3072]{1,0:T(8,128)(2,1)S(1)} collective-permute-done((bf16[256,3072]{1,0:T(8,128)(2,1)S(1)}, bf16[256,3072]{1,0:T(8,128)(2,1)S(1)}, u32[]{:S(2)}, u32[]{:S(2)}) %collective-permute-start.6) | collective-permute-done | bytes 1572896 | tf_op jit(solution)/shard_map/ppermute | solution.py:123
  441.2 27.5 %collective-permute-done.19 = bf16[256,3072]{1,0:T(8,128)(2,1)S(1)} collective-permute-done((bf16[256,3072]{1,0:T(8,128)(2,1)S(1)}, bf16[256,3072]{1,0:T(8,128)(2,1)S(1)}, u32[]{:S(2)}, u32[]{:S(2)}) %collective-permute-start.19) | collective-permute-done | bytes 1572896 | tf_op jit(solution)/shard_map/ppermute | solution.py:123
  475.8 26.6 %collective-permute-done.7 = bf16[256,3072]{1,0:T(8,128)(2,1)S(1)} collective-permute-done((bf16[256,3072]{1,0:T(8,128)(2,1)S(1)}, bf16[256,3072]{1,0:T(8,128)(2,1)S(1)}, u32[]{:S(2)}, u32[]{:S(2)}) %collective-permute-start.7) | collective-permute-done | bytes 1572896 | tf_op jit(solution)/shard_map/ppermute | solution.py:123
  509.4 26.7 %collective-permute-done.20 = bf16[256,3072]{1,0:T(8,128)(2,1)S(1)} collective-permute-done((bf16[256,3072]{1,0:T(8,128)(2,1)S(1)}, bf16[256,3072]{1,0:T(8,128)(2,1)S(1)}, u32[]{:S(2)}, u32[]{:S(2)}) %collective-permute-start.20) | collective-permute-done | bytes 1572896 | tf_op jit(solution)/shard_map/ppermute | solution.py:123
  537.4 26.5 %collective-permute-done.8 = bf16[256,3072]{1,0:T(8,128)(2,1)S(1)} collective-permute-done((bf16[256,3072]{1,0:T(8,128)(2,1)S(1)}, bf16[256,3072]{1,0:T(8,128)(2,1)S(1)}, u32[]{:S(2)}, u32[]{:S(2)}) %collective-permute-start.8) | collective-permute-done | bytes 1572896 | tf_op jit(solution)/shard_map/ppermute | solution.py:123
  (115 shorter events, 69.2 us)
Async XLA Ops:
  7.2 228.1 %all-gather.3.cloned.1.call-start = ((), (), s32[]{:S(2)}) async-start(), calls=%async_computation.2 | async-start | bytes 15925248 | tf_op jit(solution)/shard_map/all_gather | solution.py:144
  11.2 264.8 %all-gather.5.cloned.1.call-start = ((), (), s32[]{:S(2)}) async-start(), calls=%async_computation.3 | async-start | bytes 5308416 | tf_op jit(solution)/shard_map/all_gather | solution.py:145
  12.8 39.3 %collective-permute-start.1 = (bf16[256,3072]{1,0:T(8,128)(2,1)S(1)}, bf16[256,3072]{1,0:T(8,128)(2,1)S(1)}, u32[]{:S(2)}, u32[]{:S(2)}) collective-permute-start(bf16[256,3072]{1,0:T(8,128)(2,1)S(1)} %fusion.4), channel_id=1, source_target_pairs={{1,0},{2,1},{3,2},{5,4},{6,5},{7,6},{9,8},{10,9},{11,10},{13,12},{... | collective-permute-start | bytes 4718600 | tf_op jit(solution)/shard_map/ppermute | solution.py:105
  14.1 39.3 %collective-permute-start = (bf16[256,3072]{1,0:T(8,128)(2,1)S(1)}, bf16[256,3072]{1,0:T(8,128)(2,1)S(1)}, u32[]{:S(2)}, u32[]{:S(2)}) collective-permute-start(bf16[256,3072]{1,0:T(8,128)(2,1)S(1)} %fusion.4), channel_id=1, source_target_pairs={{0,1},{1,2},{2,3},{4,5},{5,6},{6,7},{8,9},{9,10},{10,11},{12,13},{... | collective-permute-start | bytes 4718600 | tf_op jit(solution)/shard_map/ppermute | solution.py:103
  52.1 37.5 %collective-permute-start.2 = (bf16[256,3072]{1,0:T(8,128)(2,1)S(1)}, bf16[256,3072]{1,0:T(8,128)(2,1)S(1)}, u32[]{:S(2)}, u32[]{:S(2)}) collective-permute-start(bf16[256,3072]{1,0:T(8,128)(2,1)S(1)} %collective-permute-done.1), channel_id=1, source_target_pairs={{1,0},{2,1},{5,4},{6,5},{9,8},{10,9},{13,12},{14,13},{17,16},{18,1... | collective-permute-start | bytes 4718600 | tf_op jit(solution)/shard_map/ppermute | solution.py:105
  53.4 37.4 %collective-permute-start.4 = (bf16[256,3072]{1,0:T(8,128)(2,1)S(1)}, bf16[256,3072]{1,0:T(8,128)(2,1)S(1)}, u32[]{:S(2)}, u32[]{:S(2)}) collective-permute-start(bf16[256,3072]{1,0:T(8,128)(2,1)S(1)} %collective-permute-done), channel_id=1, source_target_pairs={{1,2},{2,3},{5,6},{6,7},{9,10},{10,11},{13,14},{14,15},{17,18},{18... | collective-permute-start | bytes 4718600 | tf_op jit(solution)/shard_map/ppermute | solution.py:103
  89.5 36.6 %collective-permute-start.3 = (bf16[256,3072]{1,0:T(8,128)(2,1)S(1)}, bf16[256,3072]{1,0:T(8,128)(2,1)S(1)}, u32[]{:S(2)}, u32[]{:S(2)}) collective-permute-start(bf16[256,3072]{1,0:T(8,128)(2,1)S(1)} %collective-permute-done.2), channel_id=1, source_target_pairs={{1,0},{5,4},{9,8},{13,12},{17,16},{21,20},{25,24},{29,28}} | collective-permute-start | bytes 4718600 | tf_op jit(solution)/shard_map/ppermute | solution.py:105
  90.9 35.3 %collective-permute-start.5 = (bf16[256,3072]{1,0:T(8,128)(2,1)S(1)}, bf16[256,3072]{1,0:T(8,128)(2,1)S(1)}, u32[]{:S(2)}, u32[]{:S(2)}) collective-permute-start(bf16[256,3072]{1,0:T(8,128)(2,1)S(1)} %collective-permute-done.4), channel_id=1, source_target_pairs={{2,3},{6,7},{10,11},{14,15},{18,19},{22,23},{26,27},{30,31}} | collective-permute-start | bytes 4718600 | tf_op jit(solution)/shard_map/ppermute | solution.py:103
  126.2 35.8 %collective-permute-start.13 = (bf16[256,3072]{1,0:T(8,128)(2,1)S(1)}, bf16[256,3072]{1,0:T(8,128)(2,1)}, u32[]{:S(2)}, u32[]{:S(2)}) collective-permute-start(bf16[256,3072]{1,0:T(8,128)(2,1)S(1)} %copy-done.5), channel_id=1, source_target_pairs={{1,0},{2,1},{3,2},{5,4},{6,5},{7,6},{9,8},{10,9},{11,10},{13,12},{... | collective-permute-start | bytes 4718600 | tf_op jit(solution)/shard_map/ppermute | solution.py:105
  127.5 38.6 %collective-permute-start.12 = (bf16[256,3072]{1,0:T(8,128)(2,1)S(1)}, bf16[256,3072]{1,0:T(8,128)(2,1)}, u32[]{:S(2)}, u32[]{:S(2)}) collective-permute-start(bf16[256,3072]{1,0:T(8,128)(2,1)S(1)} %copy-done.5), channel_id=1, source_target_pairs={{0,1},{1,2},{2,3},{4,5},{5,6},{6,7},{8,9},{9,10},{10,11},{12,13},{... | collective-permute-start | bytes 4718600 | tf_op jit(solution)/shard_map/ppermute | solution.py:103
  133.3 434.8 %reduce-scatter.5.cloned.1.call-start = ((), (), s32[]{:S(2)}) async-start(), calls=%async_computation.5 | async-start | bytes 5308416 | tf_op jit(solution)/shard_map/reduce_scatter | solution.py:177
  162.1 35.0 %collective-permute-start.14 = (bf16[256,3072]{1,0:T(8,128)(2,1)}, bf16[256,3072]{1,0:T(8,128)(2,1)S(1)}, u32[]{:S(2)}, u32[]{:S(2)}) collective-permute-start(bf16[256,3072]{1,0:T(8,128)(2,1)} %collective-permute-done.13), channel_id=1, source_target_pairs={{1,0},{2,1},{5,4},{6,5},{9,8},{10,9},{13,12},{14,13},{17,16},{18,1... | collective-permute-start | bytes 4718600 | tf_op jit(solution)/shard_map/ppermute | solution.py:105
  275.7 294.6 %reduce-scatter.3.cloned.1.call-start = ((), (), s32[]{:S(2)}) async-start(), calls=%async_computation.4 | async-start | bytes 15925248 | tf_op jit(solution)/shard_map/reduce_scatter | solution.py:179
  363.6 37.6 %collective-permute-start.18 = (bf16[256,3072]{1,0:T(8,128)(2,1)S(1)}, bf16[256,3072]{1,0:T(8,128)(2,1)S(1)}, u32[]{:S(2)}, u32[]{:S(2)}) collective-permute-start(bf16[256,3072]{1,0:T(8,128)(2,1)S(1)} %get-tuple-element.20), channel_id=1, source_target_pairs={{0,1},{4,5},{8,9},{12,13},{16,17},{20,21},{24,25},{28,29}} | collective-permute-start | bytes 4718600 | tf_op jit(solution)/shard_map/ppermute | solution.py:123
  375.4 59.5 %collective-permute-start.6 = (bf16[256,3072]{1,0:T(8,128)(2,1)S(1)}, bf16[256,3072]{1,0:T(8,128)(2,1)S(1)}, u32[]{:S(2)}, u32[]{:S(2)}) collective-permute-start(bf16[256,3072]{1,0:T(8,128)(2,1)S(1)} %get-tuple-element.26), channel_id=1, source_target_pairs={{0,1},{4,5},{8,9},{12,13},{16,17},{20,21},{24,25},{28,29}} | collective-permute-start | bytes 4718600 | tf_op jit(solution)/shard_map/ppermute | solution.py:123
  376.8 58.1 %collective-permute-start.9 = (bf16[256,3072]{1,0:T(8,128)(2,1)S(1)}, bf16[256,3072]{1,0:T(8,128)(2,1)S(1)}, u32[]{:S(2)}, u32[]{:S(2)}) collective-permute-start(bf16[256,3072]{1,0:T(8,128)(2,1)S(1)} %get-tuple-element.27), channel_id=1, source_target_pairs={{3,2},{7,6},{11,10},{15,14},{19,18},{23,22},{27,26},{31,30}} | collective-permute-start | bytes 4718600 | tf_op jit(solution)/shard_map/ppermute | solution.py:126
  402.2 66.4 %collective-permute-start.19 = (bf16[256,3072]{1,0:T(8,128)(2,1)S(1)}, bf16[256,3072]{1,0:T(8,128)(2,1)S(1)}, u32[]{:S(2)}, u32[]{:S(2)}) collective-permute-start(bf16[256,3072]{1,0:T(8,128)(2,1)S(1)} %get-tuple-element.18), channel_id=1, source_target_pairs={{0,1},{1,2},{4,5},{5,6},{8,9},{9,10},{12,13},{13,14},{16,17},{17,1... | collective-permute-start | bytes 4718600 | tf_op jit(solution)/shard_map/ppermute | solution.py:123
  406.7 61.9 %collective-permute-start.22 = (bf16[256,3072]{1,0:T(8,128)(2,1)S(1)}, bf16[256,3072]{1,0:T(8,128)(2,1)S(1)}, u32[]{:S(2)}, u32[]{:S(2)}) collective-permute-start(bf16[256,3072]{1,0:T(8,128)(2,1)S(1)} %get-tuple-element.19), channel_id=1, source_target_pairs={{2,1},{3,2},{6,5},{7,6},{10,9},{11,10},{14,13},{15,14},{18,17},{19... | collective-permute-start | bytes 4718600 | tf_op jit(solution)/shard_map/ppermute | solution.py:126
  435.9 66.4 %collective-permute-start.7 = (bf16[256,3072]{1,0:T(8,128)(2,1)S(1)}, bf16[256,3072]{1,0:T(8,128)(2,1)S(1)}, u32[]{:S(2)}, u32[]{:S(2)}) collective-permute-start(bf16[256,3072]{1,0:T(8,128)(2,1)S(1)} %get-tuple-element.24), channel_id=1, source_target_pairs={{0,1},{1,2},{4,5},{5,6},{8,9},{9,10},{12,13},{13,14},{16,17},{17,1... | collective-permute-start | bytes 4718600 | tf_op jit(solution)/shard_map/ppermute | solution.py:123
  440.4 61.9 %collective-permute-start.10 = (bf16[256,3072]{1,0:T(8,128)(2,1)S(1)}, bf16[256,3072]{1,0:T(8,128)(2,1)S(1)}, u32[]{:S(2)}, u32[]{:S(2)}) collective-permute-start(bf16[256,3072]{1,0:T(8,128)(2,1)S(1)} %get-tuple-element.25), channel_id=1, source_target_pairs={{2,1},{3,2},{6,5},{7,6},{10,9},{11,10},{14,13},{15,14},{18,17},{19... | collective-permute-start | bytes 4718600 | tf_op jit(solution)/shard_map/ppermute | solution.py:126
  469.9 66.2 %collective-permute-start.20 = (bf16[256,3072]{1,0:T(8,128)(2,1)S(1)}, bf16[256,3072]{1,0:T(8,128)(2,1)S(1)}, u32[]{:S(2)}, u32[]{:S(2)}) collective-permute-start(bf16[256,3072]{1,0:T(8,128)(2,1)S(1)} %get-tuple-element.16), channel_id=1, source_target_pairs={{0,1},{1,2},{2,3},{4,5},{5,6},{6,7},{8,9},{9,10},{10,11},{12,13},{... | collective-permute-start | bytes 4718600 | tf_op jit(solution)/shard_map/ppermute | solution.py:123
  474.4 61.7 %collective-permute-start.23 = (bf16[256,3072]{1,0:T(8,128)(2,1)S(1)}, bf16[256,3072]{1,0:T(8,128)(2,1)S(1)}, u32[]{:S(2)}, u32[]{:S(2)}) collective-permute-start(bf16[256,3072]{1,0:T(8,128)(2,1)S(1)} %get-tuple-element.17), channel_id=1, source_target_pairs={{1,0},{2,1},{3,2},{5,4},{6,5},{7,6},{9,8},{10,9},{11,10},{13,12},{... | collective-permute-start | bytes 4718600 | tf_op jit(solution)/shard_map/ppermute | solution.py:126
  503.6 60.3 %collective-permute-start.8 = (bf16[256,3072]{1,0:T(8,128)(2,1)S(1)}, bf16[256,3072]{1,0:T(8,128)(2,1)S(1)}, u32[]{:S(2)}, u32[]{:S(2)}) collective-permute-start(bf16[256,3072]{1,0:T(8,128)(2,1)S(1)} %get-tuple-element.22), channel_id=1, source_target_pairs={{0,1},{1,2},{2,3},{4,5},{5,6},{6,7},{8,9},{9,10},{10,11},{12,13},{... | collective-permute-start | bytes 4718600 | tf_op jit(solution)/shard_map/ppermute | solution.py:123
  508.1 55.8 %collective-permute-start.11 = (bf16[256,3072]{1,0:T(8,128)(2,1)S(1)}, bf16[256,3072]{1,0:T(8,128)(2,1)S(1)}, u32[]{:S(2)}, u32[]{:S(2)}) collective-permute-start(bf16[256,3072]{1,0:T(8,128)(2,1)S(1)} %get-tuple-element.23), channel_id=1, source_target_pairs={{1,0},{2,1},{3,2},{5,4},{6,5},{7,6},{9,8},{10,9},{11,10},{13,12},{... | collective-permute-start | bytes 4718600 | tf_op jit(solution)/shard_map/ppermute | solution.py:126
  (28 other events, 1129.9 us)
Sparse Core Ops, SparseCore 0:
  11.3 84.1 all-gather.2
  133.4 40.3 all-gather.4
  275.8 55.1 reduce-scatter.4
  344.6 101.8 reduce-scatter.2

commit v2 on v1

--- a/solution.py
+++ b/solution.py
@@ -95,41 +95,49 @@
     )(projected, grad_context)
 
 
-def line_gather(block, axis, count):
+def after(value, *others):
+    return lax.optimization_barrier((value,) + others)[0]
+
+
+def line_gather(block, axis, count, ties):
     me = lax.axis_index(axis)
     right, left = [block], [block]
     for step in range(1, count):
+        rightward, leftward = right[-1], left[-1]
+        if step in ties:
+            rightward, leftward, _ = lax.optimization_barrier((rightward, leftward, ties[step]))
         right.append(
-            lax.ppermute(right[-1], axis, [(i, i + 1) for i in range(step - 1, count - 1)])
+            lax.ppermute(rightward, axis, [(i, i + 1) for i in range(step - 1, count - 1)])
         )
-        left.append(lax.ppermute(left[-1], axis, [(i, i - 1) for i in range(1, count - step + 1)]))
+        left.append(lax.ppermute(leftward, axis, [(i, i - 1) for i in range(1, count - step + 1)]))
     blocks = [block]
     for k in range(1, count):
         blocks.append(jnp.where(me >= k, right[k], left[count - k]))
     return blocks, (right[-1], left[-1])
 
 
-def line_scatter_sum(parts, axis, count):
-    from_left = from_right = None
+def line_scatter_sum(parts, axis, count, ties):
+    arrived = []
     for step in range(1, count):
         rightward, leftward = parts[step], parts[count - step]
         if step > 1:
+            from_left, from_right = arrived[-1]
             rightward = (rightward.astype(jnp.float32) + from_left.astype(jnp.float32)).astype(
                 jnp.bfloat16
             )
             leftward = (leftward.astype(jnp.float32) + from_right.astype(jnp.float32)).astype(
                 jnp.bfloat16
             )
-        from_left = lax.ppermute(
-            rightward, axis, [(i, i + 1) for i in range(0, min(step, count - 1))]
-        )
-        from_right = lax.ppermute(
-            leftward, axis, [(i, i - 1) for i in range(max(count - step, 1), count)]
-        )
+        if step in ties:
+            rightward, leftward, _ = lax.optimization_barrier((rightward, leftward, ties[step]))
+        arrived.append((
+            lax.ppermute(rightward, axis, [(i, i + 1) for i in range(0, min(step, count - 1))]),
+            lax.ppermute(leftward, axis, [(i, i - 1) for i in range(max(count - step, 1), count)]),
+        ))
     total = parts[0].astype(jnp.float32)
-    if from_left is not None:
-        total = total + from_left.astype(jnp.float32) + from_right.astype(jnp.float32)
-    return total
+    if arrived:
+        total = total + arrived[-1][0].astype(jnp.float32) + arrived[-1][1].astype(jnp.float32)
+    return total, arrived
 
 
 def per_device(count, inputs, w_qkv, w_out, upstream):
@@ -142,7 +150,7 @@
     normed_local = standard.astype(jnp.bfloat16)
 
     qkv_matrix = lax.all_gather(w_qkv, "dp", axis=0, tiled=True).reshape(width, 3 * local_width)
-    out_turned = lax.all_gather(w_out.T, "dp", axis=0, tiled=True)
+    out_cols = lax.all_gather(after(w_out, qkv_matrix), "dp", axis=1, tiled=True)
 
     def turned(blocks):
         if local_rows % PATCH == 0:
@@ -153,39 +161,44 @@
             for k in range(count)
         ]
 
-    normed_blocks, last = line_gather(normed_local, "mp", count)
+    normed_blocks, last = line_gather(normed_local, "mp", count, {})
     normed = jnp.concatenate(turned(normed_blocks), axis=0)
-    upstream_later, _, _ = lax.optimization_barrier((upstream,) + last)
-    cotangent_blocks, _ = line_gather(upstream_later, "mp", count)
+    projected = dot(normed, qkv_matrix, NN).astype(jnp.bfloat16)
+    context = attention_forward(projected)
+    attended_parts = dot(context, out_cols, NN).astype(jnp.bfloat16)
+
+    cotangent_blocks, _ = line_gather(
+        upstream, "mp", count, {1: last, 2: projected, 3: attended_parts}
+    )
     cotangent = jnp.concatenate(turned(cotangent_blocks), axis=0)
 
     def by_block(rows):
         return turned([rows[k * local_rows:(k + 1) * local_rows] for k in range(count)])
 
-    projected = dot(normed, qkv_matrix, NN).astype(jnp.bfloat16)
-    context = attention_forward(projected)
-    attended_parts = dot(context, out_turned, NT).astype(jnp.bfloat16)
-    attended = line_scatter_sum(by_block(attended_parts), "mp", count)
+    attended, arrived = line_scatter_sum(by_block(attended_parts), "mp", count, {})
     layer_out = (inputs_float + attended).astype(jnp.bfloat16)
 
-    grad_context = dot(cotangent, out_turned, NN).astype(jnp.bfloat16)
-    grad_projected = attention_backward(projected, grad_context)
+    cotangent = after(cotangent, *arrived[:1])
+    grad_context = dot(cotangent, out_cols, NT).astype(jnp.bfloat16)
+    grad_projected = after(attention_backward(projected, grad_context), *arrived[1:2])
     normed_parts = dot(grad_projected, qkv_matrix, NT).astype(jnp.bfloat16)
-    grad_normed = line_scatter_sum(by_block(normed_parts), "mp", count)
+    grad_normed, _ = line_scatter_sum(by_block(normed_parts), "mp", count, {2: arrived})
 
     out_term = dot(cotangent, context, TN).astype(jnp.bfloat16)
     out_sum = lax.psum_scatter(out_term, "dp", scatter_dimension=0, tiled=True)
-    qkv_term = dot(normed, grad_projected, TN).astype(jnp.bfloat16)
-    qkv_sum = lax.psum_scatter(
-        qkv_term.reshape(width, 3, local_width), "dp", scatter_dimension=0, tiled=True
-    )
+    grad_later = after(grad_projected, normed_parts)
+    qkv_sums = []
+    for low in range(0, 3 * local_width, local_width):
+        term = dot(normed, grad_later[:, low:low + local_width], TN).astype(jnp.bfloat16)
+        qkv_sums.append(lax.psum_scatter(term, "dp", scatter_dimension=0, tiled=True))
+    qkv_sum = jnp.stack(qkv_sums, axis=1)
 
     centre_grad = jnp.mean(grad_normed, axis=1, keepdims=True)
     along = jnp.mean(grad_normed * standard, axis=1, keepdims=True)
     grad_x = (
         upstream.astype(jnp.float32) + inv_scale * (grad_normed - centre_grad - standard * along)
     ).astype(jnp.bfloat16)
-    return (layer_out, grad_x, qkv_sum.astype(jnp.bfloat16), out_sum.T.astype(jnp.bfloat16))
+    return (layer_out, grad_x, qkv_sum, out_sum.T)
 
 
 def solution(mesh):

time: 583 us -> 520 us (0.89)
  waiting for transfers between devices: 347 us -> 274 us
  local copies, waits for them, and re-layouts: 30.4 us -> 17.9 us
  other arithmetic: 22.5 us -> 33.2 us
  starting transfers between devices: 50.8 us -> 59.2 us
    ppermute x12, waiting for transfers between devices: 189 us -> 123 us  [the longest x6 122 us: line_gather(): lax.ppermute(leftward, axis, [(i, i - 1) for i in range(1, count - step +...]
    ppermute x6, waiting for transfers between devices: 158 us -> 102 us  [line_scatter_sum(): lax.ppermute(rightward, axis, [(i, i + 1) for i in range(0, min(step, cou...]
    all_gather x1, waiting for transfers between devices: 0.01 us -> 40 us  [per_device(): lax.all_gather(w_qkv, 'dp', axis=0, tiled=True)]
    reshape x1 -> x0, local copies, waits for them, and re-layouts: 18.7 us -> none  [per_device(): qkv_term.reshape(width, 3, local_width)]
    reduce_scatter x1 -> x3, waiting for transfers between devices: 0.01 us -> 6.52 us  [per_device(): lax.psum_scatter(term, 'dp', scatter_dimension=0, tiled=True)]
    unnamed x50 -> x70, local copies, waits for them, and re-layouts: 11.3 us -> 13.4 us
    dot_general x6 -> x8, matrix products: 92.4 us -> 93.2 us  [dot(): lax.dot_general(left, right, dims, preferred_element_type=jnp.float32)]
  transfers between devices with their start and end apart: 28 -> 30, of which waited for: 12 -> 15; matrix products, arithmetic and copies ran while one was open for 24% -> 24% of each run, Pallas kernels for 3% -> 4%
where the time goes in v2:
time: 520 us; the launch traced here: 512 us
  waiting for transfers between devices  274 us (53%)
  matrix products  93.2 us (18%)
  starting transfers between devices  59.2 us (11%)
  other arithmetic  33.2 us (6%)
  Pallas kernels  19.4 us (4%)
  local copies, waits for them, and re-layouts  17.9 us (3%)
  between operations  15.2 us (3%)
    ppermute x6, waiting for transfers between devices, line_gather(): lax.ppermute(leftward, axis, [(i, i - 1) for i in range(1, count - step +...  122 us
    ppermute x6, waiting for transfers between devices, line_scatter_sum(): lax.ppermute(rightward, axis, [(i, i + 1) for i in range(0, min(step, cou...  102 us
    dot_general x8, matrix products, dot(): lax.dot_general(left, right, dims, preferred_element_type=jnp.float32)  93.2 us
    all_gather x1, waiting for transfers between devices, per_device(): lax.all_gather(w_qkv, 'dp', axis=0, tiled=True)  40 us
    ppermute x6, starting transfers between devices, line_scatter_sum(): lax.ppermute(rightward, axis, [(i, i + 1) for i in range(0, min(step, cou...  27.6 us
    ppermute x6, starting transfers between devices, line_gather(): lax.ppermute(rightward, axis, [(i, i + 1) for i in range(step - 1, count...  15.6 us
    pallas_call x1, Pallas kernels, attention_backward(): pl.pallas_call(backward_kernel, grid=(rows // PATCH,), in_specs=[rows_spe...  14 us
    unnamed x70, local copies, waits for them, and re-layouts  13.4 us
  transfers between devices with their start and end apart: 30, of which 15 were waited for; matrix products, arithmetic and copies ran while one was open for 24% of the time, Pallas kernels for 4%

profile of v2, /device:TPU:0, one launch (start us, length us, event | category | flops | bytes accessed | tf_op | source)
XLA Modules:
  0.0 512.1 jit_solution(6564326741055289113)
XLA Ops:
  14.3 6.7 %collective-permute-start = (bf16[256,3072]{1,0:T(8,128)(2,1)S(1)}, bf16[256,3072]{1,0:T(8,128)(2,1)}, u32[]{:S(2)}, u32[]{:S(2)}) collective-permute-start(bf16[256,3072]{1,0:T(8,128)(2,1)S(1)} %fusion.4), channel_id=1, source_target_pairs={{0,1},{1,2},{2,3},{4,5},{5,6},{6,7},{8,9},{9,10},{10,11},{12,13},{... | collective-permute-start | bytes 4718600 | tf_op jit(solution)/shard_map/ppermute | solution.py:110
  21.0 31.3 %collective-permute-done.1 = bf16[256,3072]{1,0:T(8,128)(2,1)S(1)} collective-permute-done((bf16[256,3072]{1,0:T(8,128)(2,1)S(1)}, bf16[256,3072]{1,0:T(8,128)(2,1)S(1)}, u32[]{:S(2)}, u32[]{:S(2)}) %collective-permute-start.1) | collective-permute-done | bytes 1572896 | tf_op jit(solution)/shard_map/ppermute | solution.py:112
  55.5 40.0 %all-gather.3.cloned.1.call-done = bf16[3072,3,768]{0,2,1:T(8,128)(2,1)} async-done(((bf16[384,3,768]{0,2,1:T(8,128)(2,1)}), bf16[3072,3,768]{0,2,1:T(8,128)(2,1)}) %all-gather.3.cloned.1.call-update) | async-done | bytes 14155792 | tf_op jit(solution)/shard_map/all_gather | solution.py:152
  100.3 34.1 %collective-permute-done.3 = bf16[256,3072]{1,0:T(8,128)(2,1)} collective-permute-done((bf16[256,3072]{1,0:T(8,128)(2,1)}, bf16[256,3072]{1,0:T(8,128)(2,1)}, u32[]{:S(2)}, u32[]{:S(2)}) %collective-permute-start.3) | collective-permute-done | bytes 1572896 | tf_op jit(solution)/shard_map/ppermute | solution.py:112
  142.4 25.7 %convolution_convert_fusion.2.projected_ref = bf16[1024,2304]{1,0:T(8,128)(2,1)} fusion(bf16[3072,2304]{0,1:T(8,128)(2,1)} %bitcast.22, bf16[256,3072]{1,0:T(8,128)(2,1)} %broadcast_select_fusion.1, bf16[256,3072]{1,0:T(8,128)(2,1)S(1)} %broadcast_select_fusion.3, bf16[256,3072]{1,0:T(8,128)(2,1)} %broadcast_select_fusion.5, bf16[256,3072]{1,0:T(8,128)(2,1)} %copy-done.19), kind=kOutput, calls=%fused_computation.4 | convolution fusion | flops 14523039744 | bytes 25165824 | tf_op jit(solution)/shard_map/dot_general | solution.py:22
  169.2 6.6 %collective-permute-done.13 = bf16[256,3072]{1,0:T(8,128)(2,1)} collective-permute-done((bf16[256,3072]{1,0:T(8,128)(2,1)S(1)}, bf16[256,3072]{1,0:T(8,128)(2,1)}, u32[]{:S(2)}, u32[]{:S(2)}) %collective-permute-start.13) | collective-permute-done | bytes 1572896 | tf_op jit(solution)/shard_map/ppermute | solution.py:112
  186.9 7.6 %convolution_convert_fusion = bf16[1024,3072]{1,0:T(8,128)(2,1)S(1)} fusion(bf16[1024,768]{1,0:T(8,128)(2,1)S(1)} %attention_forward.1, bf16[768,3072]{1,0:T(8,128)(2,1)} %all-gather.5.cloned.1.call-done), kind=kOutput, calls=%fused_computation.2 | convolution fusion | flops 4834983936 | bytes 12582912 | tf_op jit(solution)/shard_map/dot_general | solution.py:22
  194.5 23.3 %collective-permute-done.15 = bf16[256,3072]{1,0:T(8,128)(2,1)} collective-permute-done((bf16[256,3072]{1,0:T(8,128)(2,1)}, bf16[256,3072]{1,0:T(8,128)(2,1)}, u32[]{:S(2)}, u32[]{:S(2)}) %collective-permute-start.15) | collective-permute-done | bytes 1572896 | tf_op jit(solution)/shard_map/ppermute | solution.py:112
  227.3 26.3 %collective-permute-done.16 = bf16[256,3072]{1,0:T(8,128)(2,1)S(1)} collective-permute-done((bf16[256,3072]{1,0:T(8,128)(2,1)}, bf16[256,3072]{1,0:T(8,128)(2,1)S(1)}, u32[]{:S(2)}, u32[]{:S(2)}) %collective-permute-start.16) | collective-permute-done | bytes 1572896 | tf_op jit(solution)/shard_map/ppermute | solution.py:112
  260.4 6.9 %convolution_convert_fusion.3 = bf16[3072,768]{1,0:T(8,128)(2,1)} fusion(bf16[1024,3072]{1,0:T(8,128)(2,1)S(1)} %pad_maximum_fusion.1, bf16[1024,768]{1,0:T(8,128)(2,1)S(1)} %attention_forward.1), kind=kOutput, calls=%fused_computation.5 | convolution fusion | flops 4834197504 | bytes 12582912 | tf_op jit(solution)/shard_map/dot_general | solution.py:22
  276.4 9.3 %convolution_convert_fusion.7.grad_context_ref = bf16[1024,768]{1,0:T(8,128)(2,1)S(1)} fusion(bf16[1024,3072]{1,0:T(8,128)(2,1)} %copy-done.7, bf16[768,3072]{1,0:T(8,128)(2,1)} %all-gather.5.cloned.1.call-done), kind=kOutput, calls=%fused_computation.38 | convolution fusion | flops 4832624640 | bytes 12582912 | tf_op jit(solution)/shard_map/dot_general | solution.py:22
  285.7 14.0 %attention_backward.1 = bf16[1024,2304]{1,0:T(8,128)(2,1)S(1)} custom-call(bf16[1024,2304]{1,0:T(8,128)(2,1)S(1)} %bitcast.15, bf16[1024,768]{1,0:T(8,128)(2,1)S(1)} %convolution_convert_fusion.7.grad_context_ref), custom_call_target="tpu_custom_call" | custom-call | flops 2013265920 | bytes 11010048 | tf_op jit(solution)/shard_map/attention_backward/pallas_call | solution.py:84
  305.1 20.0 %convolution_convert_fusion.1 = bf16[1024,3072]{1,0:T(8,128)(2,1)} fusion(bf16[1024,2304]{1,0:T(8,128)(2,1)S(1)} %attention_backward.1, bf16[3072,2304]{0,1:T(8,128)(2,1)} %bitcast.23), kind=kOutput, calls=%fused_computation.3 | convolution fusion | flops 14498660352 | bytes 25165824 | tf_op jit(solution)/shard_map/dot_general | solution.py:22
  325.2 6.8 %convolution_convert_fusion.4 = bf16[3072,768]{1,0:T(8,128)(2,1)} fusion(bf16[1024,2304]{1,0:T(8,128)(2,1)S(1)} %attention_backward.1, bf16[256,3072]{1,0:T(8,128)(2,1)S(1)} %copy-done.11, bf16[256,3072]{1,0:T(8,128)(2,1)S(1)} %copy-done.9, bf16[256,3072]{1,0:T(8,128)(2,1)S(1)} %copy-done.10, bf16[256,3072]{1,0:T(8,128)(2,1)S(1)} %copy-done.20), kind=kOutput, calls=%fused_computation.6 | convolution fusion | flops 4859363328 | bytes 12582912 | tf_op jit(solution)/shard_map/dot_general | solution.py:22
  332.3 8.8 %convolution_convert_fusion.6 = bf16[3072,768]{1,0:T(8,128)(2,1)} fusion(bf16[1024,2304]{1,0:T(8,128)(2,1)} %copy-done.1, bf16[256,3072]{1,0:T(8,128)(2,1)} %broadcast_select_fusion.1, bf16[256,3072]{1,0:T(8,128)(2,1)S(1)} %copy-done.9, bf16[256,3072]{1,0:T(8,128)(2,1)S(1)} %copy-done.10, bf16[256,3072]{1,0:T(8,128)(2,1)} %copy-done.19), kind=kOutput, calls=%fused_computation.8 | convolution fusion | flops 4859363328 | bytes 12582912 | tf_op jit(solution)/shard_map/dot_general | solution.py:22
  347.3 7.6 %collective-permute-start.18 = (bf16[256,3072]{1,0:T(8,128)(2,1)}, bf16[256,3072]{1,0:T(8,128)(2,1)}, u32[]{:S(2)}, u32[]{:S(2)}) collective-permute-start(bf16[256,3072]{1,0:T(8,128)(2,1)} %get-tuple-element.43), channel_id=1, source_target_pairs={{0,1},{4,5},{8,9},{12,13},{16,17},{20,21},{24,25},{28,29}} | collective-permute-start | bytes 4718600 | tf_op jit(solution)/shard_map/ppermute | solution.py:134
  355.0 5.5 %add_convert_fusion.3 = (bf16[256,3072]{1,0:T(8,128)(2,1)}, bf16[256,3072]{1,0:T(8,128)(2,1)}) fusion(bf16[256,3072]{1,0:T(8,128)(2,1)S(1)} %copy-done.16, bf16[1024,3072]{1,0:T(8,128)(2,1)} %copy-done.4, bf16[256,3072]{1,0:T(8,128)(2,1)S(1)} %copy-done.18), kind=kLoop, calls=%fused_computation.36 | loop fusion | flops 6291456 | bytes 9437184 | tf_op jit(solution)/shard_map/convert_element_type | solution.py:125
  364.2 8.2 %convolution_convert_fusion.5 = bf16[3072,768]{1,0:T(8,128)(2,1)} fusion(bf16[1024,2304]{1,0:T(8,128)(2,1)} %copy-done.1, bf16[256,3072]{1,0:T(8,128)(2,1)S(1)} %copy-done.12, bf16[256,3072]{1,0:T(8,128)(2,1)S(1)} %copy-done.9, bf16[256,3072]{1,0:T(8,128)(2,1)S(1)} %copy-done.10, bf16[256,3072]{1,0:T(8,128)(2,1)S(1)} %copy-done.21), kind=kOutput, calls=%fused_computation.7 | convolution fusion | flops 4859363328 | bytes 12582912 | tf_op jit(solution)/shard_map/dot_general | solution.py:22
  372.4 16.5 %collective-permute-done.18 = bf16[256,3072]{1,0:T(8,128)(2,1)} collective-permute-done((bf16[256,3072]{1,0:T(8,128)(2,1)}, bf16[256,3072]{1,0:T(8,128)(2,1)}, u32[]{:S(2)}, u32[]{:S(2)}) %collective-permute-start.18) | collective-permute-done | bytes 1572896 | tf_op jit(solution)/shard_map/ppermute | solution.py:134
  392.1 25.6 %collective-permute-done.8 = bf16[256,3072]{1,0:T(8,128)(2,1)} collective-permute-done((bf16[256,3072]{1,0:T(8,128)(2,1)}, bf16[256,3072]{1,0:T(8,128)(2,1)}, u32[]{:S(2)}, u32[]{:S(2)}) %collective-permute-start.8) | collective-permute-done | bytes 1572896 | tf_op jit(solution)/shard_map/ppermute | solution.py:134
  423.1 28.1 %collective-permute-done.20 = bf16[256,3072]{1,0:T(8,128)(2,1)S(1)} collective-permute-done((bf16[256,3072]{1,0:T(8,128)(2,1)S(1)}, bf16[256,3072]{1,0:T(8,128)(2,1)S(1)}, u32[]{:S(2)}, u32[]{:S(2)}) %collective-permute-start.20) | collective-permute-done | bytes 1572896 | tf_op jit(solution)/shard_map/ppermute | solution.py:134
  458.7 24.8 %collective-permute-done.21 = bf16[256,3072]{1,0:T(8,128)(2,1)S(1)} collective-permute-done((bf16[256,3072]{1,0:T(8,128)(2,1)S(1)}, bf16[256,3072]{1,0:T(8,128)(2,1)S(1)}, u32[]{:S(2)}, u32[]{:S(2)}) %collective-permute-start.21) | collective-permute-done | bytes 1572896 | tf_op jit(solution)/shard_map/ppermute | solution.py:134
  487.5 5.8 %fusion.9 = (bf16[256,3072]{1,0:T(8,128)(2,1)}, bf16[256,3072]{1,0:T(8,128)(2,1)}) fusion(bf16[256,3072]{1,0:T(8,128)(2,1)S(1)} %copy-done.3, bf16[256,3072]{1,0:T(8,128)(2,1)S(1)} %copy-done.6, f32[256]{0:T(256)S(1)} %get-tuple-element.52, f32[256]{0:T(256)S(1)} %get-tuple-element.53, f32[256]{0:T(256)S(1)} %copy-done.29, f32[256]{0:T(256)S(1)} %copy-done.27, ...), kind=kLoop, calls=%fused_computation.25 | loop fusion | flops 17301504 | bytes 15732736 | tf_op jit(solution)/shard_map/convert_element_type | solution.py:200
  495.4 6.5 %reduce-scatter.7.cloned.1.call-done = bf16[384,768]{1,0:T(8,128)(2,1)} async-done(((bf16[3072,768]{1,0:T(8,128)(2,1)}), bf16[384,768]{1,0:T(8,128)(2,1)}) %reduce-scatter.7.cloned.1.call-update) | async-done | bytes 589840 | tf_op jit(solution)/shard_map/reduce_scatter | solution.py:193
  (146 shorter events, 100.8 us)
Async XLA Ops:
  7.2 88.4 %all-gather.3.cloned.1.call-start = ((), (), s32[]{:S(2)}) async-start(), calls=%async_computation.4 | async-start | bytes 15925248 | tf_op jit(solution)/shard_map/all_gather | solution.py:152
  11.2 175.7 %all-gather.5.cloned.1.call-start = ((), (), s32[]{:S(2)}) async-start(), calls=%async_computation.5 | async-start | bytes 5308416 | tf_op jit(solution)/shard_map/all_gather | solution.py:153
  12.8 39.6 %collective-permute-start.1 = (bf16[256,3072]{1,0:T(8,128)(2,1)S(1)}, bf16[256,3072]{1,0:T(8,128)(2,1)S(1)}, u32[]{:S(2)}, u32[]{:S(2)}) collective-permute-start(bf16[256,3072]{1,0:T(8,128)(2,1)S(1)} %fusion.4), channel_id=1, source_target_pairs={{1,0},{2,1},{3,2},{5,4},{6,5},{7,6},{9,8},{10,9},{11,10},{13,12},{... | collective-permute-start | bytes 4718600 | tf_op jit(solution)/shard_map/ppermute | solution.py:112
  14.3 39.3 %collective-permute-start = (bf16[256,3072]{1,0:T(8,128)(2,1)S(1)}, bf16[256,3072]{1,0:T(8,128)(2,1)}, u32[]{:S(2)}, u32[]{:S(2)}) collective-permute-start(bf16[256,3072]{1,0:T(8,128)(2,1)S(1)} %fusion.4), channel_id=1, source_target_pairs={{0,1},{1,2},{2,3},{4,5},{5,6},{6,7},{8,9},{9,10},{10,11},{12,13},{... | collective-permute-start | bytes 4718600 | tf_op jit(solution)/shard_map/ppermute | solution.py:110
  52.3 43.3 %collective-permute-start.2 = (bf16[256,3072]{1,0:T(8,128)(2,1)S(1)}, bf16[256,3072]{1,0:T(8,128)(2,1)}, u32[]{:S(2)}, u32[]{:S(2)}) collective-permute-start(bf16[256,3072]{1,0:T(8,128)(2,1)S(1)} %collective-permute-done.1), channel_id=1, source_target_pairs={{1,0},{2,1},{5,4},{6,5},{9,8},{10,9},{13,12},{14,13},{17,16},{18,1... | collective-permute-start | bytes 4718600 | tf_op jit(solution)/shard_map/ppermute | solution.py:112
  53.7 43.3 %collective-permute-start.4 = (bf16[256,3072]{1,0:T(8,128)(2,1)}, bf16[256,3072]{1,0:T(8,128)(2,1)}, u32[]{:S(2)}, u32[]{:S(2)}) collective-permute-start(bf16[256,3072]{1,0:T(8,128)(2,1)} %collective-permute-done), channel_id=1, source_target_pairs={{1,2},{2,3},{5,6},{6,7},{9,10},{10,11},{13,14},{14,15},{17,18},{18... | collective-permute-start | bytes 4718600 | tf_op jit(solution)/shard_map/ppermute | solution.py:110
  95.6 397.7 %reduce-scatter.11.cloned.1.call-start = ((), (), s32[]{:S(2)}) async-start(), calls=%async_computation.9 | async-start | bytes 5308416 | tf_op jit(solution)/shard_map/reduce_scatter | solution.py:188
  95.6 38.8 %collective-permute-start.3 = (bf16[256,3072]{1,0:T(8,128)(2,1)}, bf16[256,3072]{1,0:T(8,128)(2,1)}, u32[]{:S(2)}, u32[]{:S(2)}) collective-permute-start(bf16[256,3072]{1,0:T(8,128)(2,1)} %collective-permute-done.2), channel_id=1, source_target_pairs={{1,0},{5,4},{9,8},{13,12},{17,16},{21,20},{25,24},{29,28}} | collective-permute-start | bytes 4718600 | tf_op jit(solution)/shard_map/ppermute | solution.py:112
  96.9 37.5 %collective-permute-start.5 = (bf16[256,3072]{1,0:T(8,128)(2,1)}, bf16[256,3072]{1,0:T(8,128)(2,1)}, u32[]{:S(2)}, u32[]{:S(2)}) collective-permute-start(bf16[256,3072]{1,0:T(8,128)(2,1)} %collective-permute-done.4), channel_id=1, source_target_pairs={{2,3},{6,7},{10,11},{14,15},{18,19},{22,23},{26,27},{30,31}} | collective-permute-start | bytes 4718600 | tf_op jit(solution)/shard_map/ppermute | solution.py:110
  134.4 34.8 %collective-permute-start.12 = (bf16[256,3072]{1,0:T(8,128)(2,1)S(1)}, bf16[256,3072]{1,0:T(8,128)(2,1)}, u32[]{:S(2)}, u32[]{:S(2)}) collective-permute-start(bf16[256,3072]{1,0:T(8,128)(2,1)S(1)} %copy-done.5), channel_id=1, source_target_pairs={{0,1},{1,2},{2,3},{4,5},{5,6},{6,7},{8,9},{9,10},{10,11},{12,13},{... | collective-permute-start | bytes 4718600 | tf_op jit(solution)/shard_map/ppermute | solution.py:110
  137.0 38.8 %collective-permute-start.13 = (bf16[256,3072]{1,0:T(8,128)(2,1)S(1)}, bf16[256,3072]{1,0:T(8,128)(2,1)}, u32[]{:S(2)}, u32[]{:S(2)}) collective-permute-start(bf16[256,3072]{1,0:T(8,128)(2,1)S(1)} %copy-done.5), channel_id=1, source_target_pairs={{1,0},{2,1},{3,2},{5,4},{6,5},{7,6},{9,8},{10,9},{11,10},{13,12},{... | collective-permute-start | bytes 4718600 | tf_op jit(solution)/shard_map/ppermute | solution.py:112
  177.7 40.2 %collective-permute-start.15 = (bf16[256,3072]{1,0:T(8,128)(2,1)}, bf16[256,3072]{1,0:T(8,128)(2,1)}, u32[]{:S(2)}, u32[]{:S(2)}) collective-permute-start(bf16[256,3072]{1,0:T(8,128)(2,1)} %collective-permute-done.13), channel_id=1, source_target_pairs={{1,0},{2,1},{5,4},{6,5},{9,8},{10,9},{13,12},{14,13},{17,16},{18,1... | collective-permute-start | bytes 4718600 | tf_op jit(solution)/shard_map/ppermute | solution.py:112
  217.9 35.7 %collective-permute-start.16 = (bf16[256,3072]{1,0:T(8,128)(2,1)}, bf16[256,3072]{1,0:T(8,128)(2,1)S(1)}, u32[]{:S(2)}, u32[]{:S(2)}) collective-permute-start(bf16[256,3072]{1,0:T(8,128)(2,1)} %collective-permute-done.15), channel_id=1, source_target_pairs={{1,0},{5,4},{9,8},{13,12},{17,16},{21,20},{25,24},{29,28}} | collective-permute-start | bytes 4718600 | tf_op jit(solution)/shard_map/ppermute | solution.py:112
  220.8 33.1 %collective-permute-start.17 = (bf16[256,3072]{1,0:T(8,128)(2,1)}, bf16[256,3072]{1,0:T(8,128)(2,1)S(1)}, u32[]{:S(2)}, u32[]{:S(2)}) collective-permute-start(bf16[256,3072]{1,0:T(8,128)(2,1)} %collective-permute-done.14), channel_id=1, source_target_pairs={{2,3},{6,7},{10,11},{14,15},{18,19},{22,23},{26,27},{30,31}} | collective-permute-start | bytes 4718600 | tf_op jit(solution)/shard_map/ppermute | solution.py:110
  221.8 35.5 %collective-permute-start.6 = (bf16[256,3072]{1,0:T(8,128)(2,1)S(1)}, bf16[256,3072]{1,0:T(8,128)(2,1)S(1)}, u32[]{:S(2)}, u32[]{:S(2)}) collective-permute-start(bf16[256,3072]{1,0:T(8,128)(2,1)S(1)} %get-tuple-element.48), channel_id=1, source_target_pairs={{0,1},{4,5},{8,9},{12,13},{16,17},{20,21},{24,25},{28,29}} | collective-permute-start | bytes 4718600 | tf_op jit(solution)/shard_map/ppermute | solution.py:134
  267.2 228.2 %reduce-scatter.9.cloned.1.call-start = ((), (), s32[]{:S(2)}) async-start(), calls=%async_computation.8 | async-start | bytes 5308416 | tf_op jit(solution)/shard_map/reduce_scatter | solution.py:193
  271.6 33.5 %collective-permute-start.7 = (bf16[256,3072]{1,0:T(8,128)(2,1)S(1)}, bf16[256,3072]{1,0:T(8,128)(2,1)S(1)}, u32[]{:S(2)}, u32[]{:S(2)}) collective-permute-start(bf16[256,3072]{1,0:T(8,128)(2,1)S(1)} %get-tuple-element.46), channel_id=1, source_target_pairs={{0,1},{1,2},{4,5},{5,6},{8,9},{9,10},{12,13},{13,14},{16,17},{17,1... | collective-permute-start | bytes 4718600 | tf_op jit(solution)/shard_map/ppermute | solution.py:134
  332.0 163.4 %reduce-scatter.5.cloned.1.call-start = ((), (), s32[]{:S(2)}) async-start(), calls=%async_computation.6 | async-start | bytes 5308416 | tf_op jit(solution)/shard_map/reduce_scatter | solution.py:193
  341.2 160.8 %reduce-scatter.7.cloned.1.call-start = ((), (), s32[]{:S(2)}) async-start(), calls=%async_computation.7 | async-start | bytes 5308416 | tf_op jit(solution)/shard_map/reduce_scatter | solution.py:193
  347.3 41.6 %collective-permute-start.18 = (bf16[256,3072]{1,0:T(8,128)(2,1)}, bf16[256,3072]{1,0:T(8,128)(2,1)}, u32[]{:S(2)}, u32[]{:S(2)}) collective-permute-start(bf16[256,3072]{1,0:T(8,128)(2,1)} %get-tuple-element.43), channel_id=1, source_target_pairs={{0,1},{4,5},{8,9},{12,13},{16,17},{20,21},{24,25},{28,29}} | collective-permute-start | bytes 4718600 | tf_op jit(solution)/shard_map/ppermute | solution.py:134
  360.4 57.3 %collective-permute-start.8 = (bf16[256,3072]{1,0:T(8,128)(2,1)}, bf16[256,3072]{1,0:T(8,128)(2,1)}, u32[]{:S(2)}, u32[]{:S(2)}) collective-permute-start(bf16[256,3072]{1,0:T(8,128)(2,1)} %get-tuple-element.44), channel_id=1, source_target_pairs={{0,1},{1,2},{2,3},{4,5},{5,6},{6,7},{8,9},{9,10},{10,11},{12,13},{... | collective-permute-start | bytes 4718600 | tf_op jit(solution)/shard_map/ppermute | solution.py:134
  362.9 54.9 %collective-permute-start.11 = (bf16[256,3072]{1,0:T(8,128)(2,1)}, bf16[256,3072]{1,0:T(8,128)(2,1)}, u32[]{:S(2)}, u32[]{:S(2)}) collective-permute-start(bf16[256,3072]{1,0:T(8,128)(2,1)} %get-tuple-element.45), channel_id=1, source_target_pairs={{1,0},{2,1},{3,2},{5,4},{6,5},{7,6},{9,8},{10,9},{11,10},{13,12},{... | collective-permute-start | bytes 4718600 | tf_op jit(solution)/shard_map/ppermute | solution.py:135
  417.7 33.5 %collective-permute-start.20 = (bf16[256,3072]{1,0:T(8,128)(2,1)S(1)}, bf16[256,3072]{1,0:T(8,128)(2,1)S(1)}, u32[]{:S(2)}, u32[]{:S(2)}) collective-permute-start(bf16[256,3072]{1,0:T(8,128)(2,1)S(1)} %get-tuple-element.25), channel_id=1, source_target_pairs={{0,1},{1,2},{4,5},{5,6},{8,9},{9,10},{12,13},{13,14},{16,17},{17,1... | collective-permute-start | bytes 4718600 | tf_op jit(solution)/shard_map/ppermute | solution.py:134
  452.4 31.0 %collective-permute-start.21 = (bf16[256,3072]{1,0:T(8,128)(2,1)S(1)}, bf16[256,3072]{1,0:T(8,128)(2,1)S(1)}, u32[]{:S(2)}, u32[]{:S(2)}) collective-permute-start(bf16[256,3072]{1,0:T(8,128)(2,1)S(1)} %get-tuple-element.38), channel_id=1, source_target_pairs={{0,1},{1,2},{2,3},{4,5},{5,6},{6,7},{8,9},{9,10},{10,11},{12,13},{... | collective-permute-start | bytes 4718600 | tf_op jit(solution)/shard_map/ppermute | solution.py:134
  (40 other events, 1230.7 us)
Sparse Core Ops, SparseCore 0:
  11.3 84.1 all-gather.2
  97.4 39.7 all-gather.4
  267.4 52.2 reduce-scatter.10
  332.2 54.9 reduce-scatter.8
  390.4 53.8 reduce-scatter.4
  448.0 53.8 reduce-scatter.6
